TPU v7x, 32 devices: a whole 2x2x4 slice. The times are simulated.
32 devices in a mesh: row: 8 (over z, core), col: 4 (over y, x).
Axes of the slice: x: 2, y: 2, z: 4, core: 2. Of those that a mesh axis runs over, the one named last changes fastest.
Arguments:
- snapshots: float32 [12288, 2048], P('row', 'col'), may hold values from -6 to 6
- mass: float32 [12288], P('row'), may hold values from 1 to 30, as said below
Outputs:
- gram: float32 [2048, 2048], P('col', 'row')
Inputs may be any that keep to these rules, and one draw needn't show every extreme that they name: `mass`: positive lumped masses.
All inputs are finite; a program needn't handle non-finite values.
Results may differ from a plain program's by a relative error of at most 0.00005.
Values sent between devices are 32-bit elements; how exact they have to be, the bound alone decides.
A program may use at most 128 MiB of HBM per device.

v0:
```python
import jax
import jax.numpy as jnp
from jax import lax
from jax.sharding import PartitionSpec as P


def contract(left, right):
    return lax.dot_general(
        left,
        right,
        (((0,), (0,)), ((), ())),
        precision=lax.Precision.HIGHEST,
        preferred_element_type=jnp.float32,
    )


def shards(snapshots, mass):
    total = lax.psum(jnp.sum(mass), "row")
    weighted = snapshots * mass[:, None]
    partial_rows = contract(weighted, lax.all_gather(snapshots, "col", axis=1, tiled=True))
    summed = lax.psum_scatter(partial_rows, "row", scatter_dimension=1, tiled=True)
    return summed / total


def solution(mesh):
    in_specs = (P("row", "col"), P("row"))
    out_specs = P("col", "row")
    return jax.shard_map(shards, mesh=mesh, in_specs=in_specs, out_specs=out_specs, check_vma=False)
```

profile of v0, /device:TPU:3, one launch (start us, length us, event | category | flops | bytes accessed | tf_op | source)
XLA Modules:
  0.0 216.6 jit_solution(10141281828670325992)
XLA Ops:
  6.5 0.0 all-gather.2.cloned.1.call-start
  6.5 0.7 all-gather.2.cloned.1.call-update
  7.3 0.0 reduce-scatter.2.cloned.1.call-start
  7.3 125.7 %all-gather.2.cloned.1.call-done = f32[1536,2048]{1,0:T(8,128)} async-done(((f32[1536,512]{1,0:T(8,128)}), f32[1536,2048]{1,0:T(8,128)}) %all-gather.2.cloned.1.call-update) | async-done | bytes 12582928 | tf_op jit(solution)/shard_map/all_gather | solution.py:20
  133.0 26.0 %fusion = f32[512,2048]{1,0:T(8,128)} fusion(f32[1536,2048]{1,0:T(8,128)} %all-gather.2.cloned.1.call-done, f32[1536,512]{1,0:T(8,128)} %param.2, f32[1536]{0:T(1024)} %param.3), kind=kOutput, calls=%fused_computation | convolution fusion | flops 19328139264 | bytes 19929088 | tf_op jit(solution)/shard_map/dot_general | solution.py:8
  159.0 0.0 copy-start
  159.0 0.0 reduce-scatter.2.cloned.1.call-update
  159.0 0.7 copy-done
  159.7 0.6 reduce_sum.9
  160.3 14.4 %psum.7 = f32[]{:T(128)} all-reduce(f32[]{:T(128)} %reduce_sum.9), channel_id=1, replica_groups=mesh['row'=8,'col'=4] {'row'}, use_global_device_ids=true, to_apply=%region_2.0 | all-reduce | flops 1 | bytes 8 | tf_op jit(solution)/shard_map/psum | solution.py:18
  174.7 32.5 %reduce-scatter.2.cloned.1.call-done = f32[512,256]{1,0:T(8,128)} async-done(((f32[512,2048]{1,0:T(8,128)}), f32[512,256]{1,0:T(8,128)}) %reduce-scatter.2.cloned.1.call-update) | async-done | bytes 524304 | tf_op jit(solution)/shard_map/reduce_scatter | solution.py:21
  207.2 2.6 %broadcast_divide_fusion = f32[512,256]{1,0:T(8,128)} fusion(f32[512,256]{1,0:T(8,128)} %reduce-scatter.2.cloned.1.call-done, f32[]{:T(128)} %psum.7), kind=kLoop, calls=%fused_computation.3 | loop fusion | flops 131072 | bytes 1048580 | tf_op jit(solution)/shard_map/div | solution.py:22
Async XLA Ops:
  6.5 126.4 %all-gather.2.cloned.1.call-start = ((), (), s32[]{:S(2)}) async-start(), calls=%async_computation.1 | async-start | bytes 15728640 | tf_op jit(solution)/shard_map/all_gather | solution.py:20
  7.3 200.0 %reduce-scatter.2.cloned.1.call-start = ((), (), s32[]{:S(2)}) async-start(), calls=%async_computation.2 | async-start | bytes 4718592 | tf_op jit(solution)/shard_map/reduce_scatter | solution.py:21
  159.0 0.7 copy-start
Sparse Core Ops, SparseCore 0:
  9.2 123.7 all-gather.1
  159.1 48.0 reduce-scatter.1
where the time goes:
time: 220 us; the launch traced here: 217 us
  waiting for transfers between devices  159 us (72%)
  matrix products  26 us (12%)
  blocking collectives  14.4 us (7%)
  between operations  13.4 us (6%)
  other arithmetic  3.16 us (1%)
    all_gather x1, waiting for transfers between devices, shards(): lax.all_gather(snapshots, 'col', axis=1, tiled=True)  126 us
    reduce_scatter x1, waiting for transfers between devices, shards(): lax.psum_scatter(partial_rows, 'row', scatter_dimension=1, tiled=True)  32.5 us
    dot_general x1, matrix products, contract(): lax.dot_general(left, right, (((0,), (0,)), ((), ())), precision=lax.Prec...  26 us
    psum x1, blocking collectives, shards(): total = lax.psum(jnp.sum(mass), 'row')  14.4 us
  transfers between devices with their start and end apart: 2, of which 2 were waited for; matrix products, arithmetic and copies ran while one was open for 0% of the time, Pallas kernels for 0%

commit v1 on v0

v1 whole, which is shorter than its diff:
```python
import functools

import jax
import jax.numpy as jnp
from jax import lax
from jax.experimental import pallas as pl
from jax.experimental.pallas import tpu as pltpu
from jax.sharding import PartitionSpec as P

MESH = pl.DeviceIdType.MESH
LANES = 128
EXTRA = 8


def halves(value):
    high = value.astype(jnp.bfloat16)
    low = (value - high.astype(jnp.float32)).astype(jnp.bfloat16)
    return high, low


def product(left_high, left_low, right_high, right_low):
    dot = functools.partial(jnp.dot, preferred_element_type=jnp.float32)
    return dot(left_high, right_high) + (dot(left_high, right_low) + dot(left_low, right_high))


def kernel(
    rows_n, cols_n, s_ref, mass_ref, out_ref,
    rhs, lhs_high, lhs_low, kept, given, taken, swapped, landed,
    y_send, y_recv, own_send, fwd_send, x_recv,
    core_send, core_recv, swap_send, swap_recv, z_send, z_recv,
):
    row, col = lax.axis_index("row"), lax.axis_index("col")
    lo_n, z_n = cols_n // 2, rows_n // 2
    core, z = lax.rem(row, 2), row // 2
    hi, lo = col // lo_n, lax.rem(col, lo_n)
    depth, block = s_ref.shape[0] // 2, s_ref.shape[1]
    slices = block // LANES
    width = out_ref.shape[1]
    subs = width // LANES
    per_block = block // (2 * LANES)
    units = per_block * cols_n
    z_per_block = per_block // subs

    sibling = (row + 1 - 2 * core, col)
    across = (row, (1 - hi) * lo_n + lo)

    def along(d):
        return (row, hi * lo_n + lax.rem(lo + lo_n - d, lo_n))

    def layer(other):
        return (other * 2 + core, col)

    def part(half, sl):
        return s_ref.at[pl.ds(pl.multiple_of(half * depth, depth), depth), pl.ds(sl * LANES, LANES)]

    def copy(src, dst, send, recv, device):
        return pltpu.make_async_remote_copy(
            src_ref=src, dst_ref=dst, send_sem=send, recv_sem=recv, device_id=device, device_id_type=MESH
        )

    def y_copy(sl):
        return copy(part(1 - hi, sl), rhs.at[hi, sl], y_send.at[sl], y_recv.at[sl], across)

    def own_copy(d, sl):
        at = 2 * d + hi
        return copy(part(hi, sl), rhs.at[at, sl], own_send.at[d, sl], x_recv.at[at, sl], along(d))

    def fwd_copy(d, sl):
        at = 2 * d + 1 - hi
        return copy(rhs.at[1 - hi, sl], rhs.at[at, sl], fwd_send.at[d, sl], x_recv.at[at, sl], along(d))

    def core_copy(u):
        return copy(given.at[u], taken.at[u], core_send.at[u], core_recv.at[u], sibling)

    def swap_copy(u):
        return copy(kept.at[u, 1], swapped.at[u], swap_send.at[u], swap_recv.at[u], across)

    def place(u):
        t, rest = u // cols_n, lax.rem(u, cols_n)
        d, e = rest // 2, lax.rem(rest, 2)
        which = lax.rem(e + z, 2)
        at = 2 * d + which
        col_block = which * lo_n + lax.rem(lo + d, lo_n)
        target = col_block * z_per_block + t // subs
        return t, d, at, target, lax.rem(t, subs)

    def slice_of(k, t):
        return (2 * (t // subs) + k) * subs + lax.rem(t, subs)

    def z_copy(u):
        _, _, _, target, sub = place(u)
        return copy(kept.at[u, 0], landed.at[z, sub], z_send.at[u], z_recv.at[z, sub], layer(target))

    peers = [sibling, across] + [along(d) for d in range(1, lo_n)]
    peers += [layer(lax.rem(z + d, z_n)) for d in range(1, z_n)]
    barrier = pltpu.get_barrier_semaphore()
    for peer in peers:
        pl.semaphore_signal(barrier, inc=1, device_id=peer, device_id_type=MESH)
    pl.semaphore_wait(barrier, len(peers))

    for sl in range(slices):
        y_copy(sl).start()
        for d in range(1, lo_n):
            own_copy(d, sl).start()

    mass = mass_ref[pl.ds(pl.multiple_of(hi * depth, depth), depth), :]
    summed = jnp.broadcast_to(jnp.sum(mass, axis=0, keepdims=True), (EXTRA, LANES))

    def put_left(first, sl, value):
        high, low = halves(jnp.transpose(value * mass))
        at = pl.ds(first + sl * LANES, LANES)
        lhs_high[at, :] = high
        lhs_low[at, :] = low

    for sl in range(slices):
        value = part(hi, sl)[...]
        rhs[hi, sl] = value
        put_left(0, sl, value)
    for sl in range(slices):
        y_copy(sl).wait_recv()
        for d in range(1, lo_n):
            fwd_copy(d, sl).start()
        put_left(block, sl, rhs[1 - hi, sl])

    def compute(u):
        t, d, at, _, _ = place(u)
        mine, theirs = slice_of(core, t), slice_of(1 - core, t)

        @pl.when(d > 0)
        def _():
            for sl in (mine, theirs):
                copy(rhs.at[at, sl], rhs.at[at, sl], own_send.at[0, 0], x_recv.at[at, sl], along(1)).wait_recv()

        right = jnp.concatenate([rhs[at, mine], rhs[at, theirs]], axis=1)
        high, low = halves(right)
        for side in range(2):
            at_rows = pl.ds(side * block, block)
            value = product(lhs_high[at_rows, :], lhs_low[at_rows, :], high, low)
            kept[u, side, :block, :] = value[:, :LANES]
            given[u, side, :block, :] = value[:, LANES:]
            kept[u, side, block:, :] = summed
            given[u, side, block:, :] = summed
        core_copy(u).start()

    def join_cores(u):
        core_copy(u).wait_recv()
        kept[u, 1] = kept[u, 1] + taken[u, 1]
        swap_copy(u).start()
        kept[u, 0] = kept[u, 0] + taken[u, 0]

    def join_across(u):
        _, _, _, target, sub = place(u)
        swap_copy(u).wait_recv()
        value = kept[u, 0] + swapped[u]

        @pl.when(target == z)
        def _():
            landed[z, sub] = value

        @pl.when(target != z)
        def _():
            kept[u, 0] = value
            z_copy(u).start()

    def step(i, carry):
        @pl.when(i < units)
        def _():
            compute(i)

        @pl.when((i >= 1) & (i < units + 1))
        def _():
            join_cores(i - 1)

        @pl.when(i >= 2)
        def _():
            join_across(i - 2)

        return carry

    lax.fori_loop(0, units + 2, step, 0)

    for d in range(1, z_n):
        source = lax.rem(z + d, z_n)
        for sub in range(subs):
            copy(
                landed.at[source, sub], landed.at[source, sub], z_send.at[0], z_recv.at[source, sub], layer(source)
            ).wait_recv()
    for sub in range(subs):
        value = landed[0, sub]
        for source in range(1, z_n):
            value = value + landed[source, sub]
        out_ref[:, sub * LANES : (sub + 1) * LANES] = value[:block] / value[block : block + 1]

    for sl in range(slices):
        y_copy(sl).wait_send()
        for d in range(1, lo_n):
            own_copy(d, sl).wait_send()
            fwd_copy(d, sl).wait_send()

    def drain(u, carry):
        core_copy(u).wait_send()
        swap_copy(u).wait_send()

        @pl.when(place(u)[3] != z)
        def _():
            z_copy(u).wait_send()

        return carry

    lax.fori_loop(0, units, drain, 0)


def solution(mesh):
    rows_n, cols_n = mesh.shape["row"], mesh.shape["col"]

    def shards(snapshots, mass):
        rows, block = snapshots.shape
        depth, slices, lo_n, z_n = rows // 2, block // LANES, cols_n // 2, rows_n // 2
        width = block * cols_n // rows_n
        subs = width // LANES
        units = block // (2 * LANES) * cols_n
        piece = (block + EXTRA, LANES)
        dma = pltpu.SemaphoreType.DMA
        flops = 2 * depth * 2 * block * block * cols_n * 3
        return pl.pallas_call(
            functools.partial(kernel, rows_n, cols_n),
            out_shape=jax.ShapeDtypeStruct((block, width), jnp.float32),
            in_specs=[pl.BlockSpec(memory_space=pltpu.VMEM)] * 2,
            out_specs=pl.BlockSpec(memory_space=pltpu.VMEM),
            scratch_shapes=[
                pltpu.VMEM((cols_n, slices, depth, LANES), jnp.float32),
                pltpu.VMEM((2 * block, depth), jnp.bfloat16),
                pltpu.VMEM((2 * block, depth), jnp.bfloat16),
                pltpu.VMEM((units, 2) + piece, jnp.float32),
                pltpu.VMEM((units, 2) + piece, jnp.float32),
                pltpu.VMEM((units, 2) + piece, jnp.float32),
                pltpu.VMEM((units,) + piece, jnp.float32),
                pltpu.VMEM((z_n, subs) + piece, jnp.float32),
                dma((slices,)), dma((slices,)),
                dma((lo_n, slices)), dma((lo_n, slices)), dma((cols_n, slices)),
                dma((units,)), dma((units,)), dma((units,)), dma((units,)), dma((units,)),
                dma((z_n, subs)),
            ],
            compiler_params=pltpu.CompilerParams(
                collective_id=0, has_side_effects=True, vmem_limit_bytes=62 * 1024 * 1024
            ),
            cost_estimate=pl.CostEstimate(flops=flops, bytes_accessed=4 * rows * block, transcendentals=0),
        )(snapshots, mass[:, None])

    in_specs = (P("row", "col"), P("row"))
    return jax.shard_map(shards, mesh=mesh, in_specs=in_specs, out_specs=P("col", "row"), check_vma=False)
```

time: 220 us -> 127 us (0.58); the launches traced: 217 us -> 126 us
  waiting for transfers between devices: 159 us -> 0 us
  Pallas kernels: 0 us -> 123 us
  matrix products: 26 us -> 0 us
  blocking collectives: 14.4 us -> 0 us
  between operations: 13.4 us -> 0.01 us
  other arithmetic: 3.16 us -> 0 us
  local copies, waits for them, and re-layouts: 0.67 us -> 3.71 us
    all_gather x1 -> x0, waiting for transfers between devices: 126 us -> none  [shards(): lax.all_gather(snapshots, 'col', axis=1, tiled=True)]
    pallas_call x0 -> x1, Pallas kernels: none -> 123 us  [shards(): pl.pallas_call(functools.partial(kernel, rows_n, cols_n), out_shape=jax.S...]
    reduce_scatter x1 -> x0, waiting for transfers between devices: 32.5 us -> none  [shards(): lax.psum_scatter(partial_rows, 'row', scatter_dimension=1, tiled=True)]
    dot_general x1 -> x0, matrix products: 26 us -> none  [contract(): lax.dot_general(left, right, (((0,), (0,)), ((), ())), precision=lax.Prec...]
    psum x1 -> x0, blocking collectives: 14.4 us -> none  [shards(): total = lax.psum(jnp.sum(mass), 'row')]
    div x1 -> x0, other arithmetic: 2.56 us -> none  [shards(): return summed / total]
  transfers between devices with their start and end apart: 2 -> 0, of which waited for: 2 -> 0; matrix products, arithmetic and copies ran while one was open for 0% -> 0% of each run, Pallas kernels for 0% -> 0%
where the time goes in v1:
time: 127 us; the launch traced here: 126 us
  Pallas kernels  123 us (97%)
  local copies, waits for them, and re-layouts  3.71 us (3%)
    pallas_call x1, Pallas kernels, shards(): pl.pallas_call(functools.partial(kernel, rows_n, cols_n), out_shape=jax.S...  123 us

profile of v1, /device:TPU:3, one launch (start us, length us, event | category | flops | bytes accessed | tf_op | source)
XLA Modules:
  0.0 126.5 jit_solution(8566602762641319673)
XLA Ops:
  0.0 1.8 %broadcast_in_dim.4.mass_ref = f32[1536,1]{1,0:T(8,128)} reshape(f32[1536]{0:T(1024)} %param.3) | data formatting | bytes 12288 | tf_op jit(solution)/shard_map/broadcast_in_dim | solution.py:248
  1.8 122.8 %shard_map.28 = f32[512,256]{1,0:T(8,128)} custom-call(f32[1536,512]{1,0:T(8,128)} %s_ref.1, f32[1536,1]{1,0:T(8,128)} %broadcast_in_dim.4.mass_ref), custom_call_target="tpu_custom_call" | custom-call | flops 9663676416 | bytes 3145728 | tf_op jit(solution)/shard_map/pallas_call | solution.py:225
  124.6 1.9 %copy.5 = f32[512,256]{1,0:T(8,128)} copy(f32[512,256]{1,0:T(8,128)} %shard_map.28) | data formatting | bytes 1048576

commit v2 on v1

--- a/solution.py
+++ b/solution.py
@@ -26,7 +26,7 @@
 def kernel(
     rows_n, cols_n, s_ref, mass_ref, out_ref,
     rhs, lhs_high, lhs_low, kept, given, taken, swapped, landed,
-    y_send, y_recv, own_send, fwd_send, x_recv,
+    load_sem, y_send, y_recv, own_send, fwd_send, x_recv,
     core_send, core_recv, swap_send, swap_recv, z_send, z_recv,
 ):
     row, col = lax.axis_index("row"), lax.axis_index("col")
@@ -85,7 +85,7 @@
         return t, d, at, target, lax.rem(t, subs)
 
     def slice_of(k, t):
-        return (2 * (t // subs) + k) * subs + lax.rem(t, subs)
+        return (2 * (t // subs) + k) * subs + t % subs
 
     def z_copy(u):
         _, _, _, target, sub = place(u)
@@ -98,27 +98,38 @@
         pl.semaphore_signal(barrier, inc=1, device_id=peer, device_id_type=MESH)
     pl.semaphore_wait(barrier, len(peers))
 
-    for sl in range(slices):
+    def load(sl):
+        return pltpu.make_async_copy(part(hi, sl), rhs.at[hi, sl], load_sem.at[sl])
+
+    order = [slice_of(k, t) for t in range(per_block) for k in range(2)]
+    ahead = 2
+    for sl in order[:ahead]:
         y_copy(sl).start()
         for d in range(1, lo_n):
             own_copy(d, sl).start()
-
-    mass = mass_ref[pl.ds(pl.multiple_of(hi * depth, depth), depth), :]
-    summed = jnp.broadcast_to(jnp.sum(mass, axis=0, keepdims=True), (EXTRA, LANES))
+    for sl in order:
+        load(sl).start()
+
+    mass = mass_ref[:, pl.ds(pl.multiple_of(hi * depth, depth), depth)]
+    summed = jnp.broadcast_to(jnp.sum(mass, axis=1, keepdims=True), (EXTRA, LANES))
 
     def put_left(first, sl, value):
-        high, low = halves(jnp.transpose(value * mass))
+        high, low = halves(jnp.transpose(value) * mass)
         at = pl.ds(first + sl * LANES, LANES)
         lhs_high[at, :] = high
         lhs_low[at, :] = low
 
-    for sl in range(slices):
-        value = part(hi, sl)[...]
-        rhs[hi, sl] = value
-        put_left(0, sl, value)
-    for sl in range(slices):
+    for sl in order:
+        load(sl).wait()
+        put_left(0, sl, rhs[hi, sl])
+    for n, sl in enumerate(order):
+        y_copy(sl).wait_send()
+        if n + ahead < slices:
+            y_copy(order[n + ahead]).start()
         y_copy(sl).wait_recv()
         for d in range(1, lo_n):
+            if n >= ahead:
+                own_copy(d, sl).start()
             fwd_copy(d, sl).start()
         put_left(block, sl, rhs[1 - hi, sl])
 
@@ -163,17 +174,14 @@
             z_copy(u).start()
 
     def step(i, carry):
+        @pl.when(i >= 2)
+        def _():
+            join_across(i - 2)
+
         @pl.when(i < units)
         def _():
             compute(i)
-
-        @pl.when((i >= 1) & (i < units + 1))
-        def _():
-            join_cores(i - 1)
-
-        @pl.when(i >= 2)
-        def _():
-            join_across(i - 2)
+            join_cores(i)
 
         return carry
 
@@ -192,7 +200,6 @@
         out_ref[:, sub * LANES : (sub + 1) * LANES] = value[:block] / value[block : block + 1]
 
     for sl in range(slices):
-        y_copy(sl).wait_send()
         for d in range(1, lo_n):
             own_copy(d, sl).wait_send()
             fwd_copy(d, sl).wait_send()
@@ -225,7 +232,7 @@
         return pl.pallas_call(
             functools.partial(kernel, rows_n, cols_n),
             out_shape=jax.ShapeDtypeStruct((block, width), jnp.float32),
-            in_specs=[pl.BlockSpec(memory_space=pltpu.VMEM)] * 2,
+            in_specs=[pl.BlockSpec(memory_space=pl.ANY), pl.BlockSpec(memory_space=pltpu.VMEM)],
             out_specs=pl.BlockSpec(memory_space=pltpu.VMEM),
             scratch_shapes=[
                 pltpu.VMEM((cols_n, slices, depth, LANES), jnp.float32),
@@ -236,7 +243,7 @@
                 pltpu.VMEM((units, 2) + piece, jnp.float32),
                 pltpu.VMEM((units,) + piece, jnp.float32),
                 pltpu.VMEM((z_n, subs) + piece, jnp.float32),
-                dma((slices,)), dma((slices,)),
+                dma((slices,)), dma((slices,)), dma((slices,)),
                 dma((lo_n, slices)), dma((lo_n, slices)), dma((cols_n, slices)),
                 dma((units,)), dma((units,)), dma((units,)), dma((units,)), dma((units,)),
                 dma((z_n, subs)),
@@ -245,7 +252,7 @@
                 collective_id=0, has_side_effects=True, vmem_limit_bytes=62 * 1024 * 1024
             ),
             cost_estimate=pl.CostEstimate(flops=flops, bytes_accessed=4 * rows * block, transcendentals=0),
-        )(snapshots, mass[:, None])
+        )(snapshots, mass[None, :])
 
     in_specs = (P("row", "col"), P("row"))
     return jax.shard_map(shards, mesh=mesh, in_specs=in_specs, out_specs=P("col", "row"), check_vma=False)

time: 127 us -> 109 us (0.86)
  Pallas kernels: 123 us -> 106 us
    pallas_call x1, Pallas kernels: 123 us -> 106 us  [shards(): pl.pallas_call(functools.partial(kernel, rows_n, cols_n), out_shape=jax.S...]
where the time goes in v2:
time: 109 us
  Pallas kernels  106 us (97%)
  local copies, waits for them, and re-layouts  3.16 us (3%)
    pallas_call x1, Pallas kernels, shards(): pl.pallas_call(functools.partial(kernel, rows_n, cols_n), out_shape=jax.S...  106 us

profile of v2, /device:TPU:3, one launch (start us, length us, event | category | flops | bytes accessed | tf_op | source)
XLA Modules:
  0.0 109.1 jit_solution(11278228530865461646)
XLA Ops:
  0.0 1.3 %broadcast_in_dim.3.mass_ref = f32[1,1536]{1,0:T(1,128)} reshape(f32[1536]{0:T(1024)} %param.3) | data formatting | bytes 12288 | tf_op jit(solution)/shard_map/broadcast_in_dim | solution.py:255
  1.3 105.9 %shard_map.28 = f32[512,256]{1,0:T(8,128)} custom-call(f32[1536,512]{1,0:T(8,128)} %s_ref.1, f32[1,1536]{1,0:T(1,128)} %broadcast_in_dim.3.mass_ref), custom_call_target="tpu_custom_call" | custom-call | flops 9663676416 | bytes 3145728 | tf_op jit(solution)/shard_map/pallas_call | solution.py:232
  107.2 1.9 %copy.4 = f32[512,256]{1,0:T(8,128)} copy(f32[512,256]{1,0:T(8,128)} %shard_map.28) | data formatting | bytes 1048576

commit v3 on v2

--- a/solution.py
+++ b/solution.py
@@ -10,6 +10,8 @@
 MESH = pl.DeviceIdType.MESH
 LANES = 128
 EXTRA = 8
+SPLIT = 2
+LATER = 2
 
 
 def halves(value):
@@ -41,6 +43,8 @@
     units = per_block * cols_n
     z_per_block = per_block // subs
 
+    first = lax.rem(1 + z // 2, 2)
+
     sibling = (row + 1 - 2 * core, col)
     across = (row, (1 - hi) * lo_n + lo)
 
@@ -69,16 +73,19 @@
         at = 2 * d + 1 - hi
         return copy(rhs.at[1 - hi, sl], rhs.at[at, sl], fwd_send.at[d, sl], x_recv.at[at, sl], along(d))
 
-    def core_copy(u):
-        return copy(given.at[u], taken.at[u], core_send.at[u], core_recv.at[u], sibling)
-
-    def swap_copy(u):
-        return copy(kept.at[u, 1], swapped.at[u], swap_send.at[u], swap_recv.at[u], across)
+    edges = [0] + [(block // SPLIT) * (h + 1) for h in range(SPLIT - 1)] + [block + EXTRA]
+    spans = [pl.ds(edges[h], edges[h + 1] - edges[h]) for h in range(SPLIT)]
+
+    def core_copy(u, side):
+        return copy(given.at[u, side], taken.at[u, side], core_send.at[u, side], core_recv.at[u, side], sibling)
+
+    def swap_copy(u, h):
+        return copy(kept.at[u, 1, spans[h]], swapped.at[u, spans[h]], swap_send.at[u, h], swap_recv.at[u, h], across)
 
     def place(u):
         t, rest = u // cols_n, lax.rem(u, cols_n)
         d, e = rest // 2, lax.rem(rest, 2)
-        which = lax.rem(e + z, 2)
+        which = lax.rem(e + first, 2)
         at = 2 * d + which
         col_block = which * lo_n + lax.rem(lo + d, lo_n)
         target = col_block * z_per_block + t // subs
@@ -87,9 +94,11 @@
     def slice_of(k, t):
         return (2 * (t // subs) + k) * subs + t % subs
 
-    def z_copy(u):
+    def z_copy(u, h):
         _, _, _, target, sub = place(u)
-        return copy(kept.at[u, 0], landed.at[z, sub], z_send.at[u], z_recv.at[z, sub], layer(target))
+        return copy(
+            kept.at[u, 0, spans[h]], landed.at[z, sub, spans[h]], z_send.at[u, h], z_recv.at[z, sub, h], layer(target)
+        )
 
     peers = [sibling, across] + [along(d) for d in range(1, lo_n)]
     peers += [layer(lax.rem(z + d, z_n)) for d in range(1, z_n)]
@@ -122,15 +131,27 @@
     for sl in order:
         load(sl).wait()
         put_left(0, sl, rhs[hi, sl])
+    def send_later(sl, own):
+        @pl.when(own)
+        def _():
+            for d in range(1, lo_n):
+                own_copy(d, sl).start()
+
+        @pl.when(jnp.logical_not(own))
+        def _():
+            for d in range(1, lo_n):
+                fwd_copy(d, sl).start()
+
     for n, sl in enumerate(order):
         y_copy(sl).wait_send()
         if n + ahead < slices:
             y_copy(order[n + ahead]).start()
         y_copy(sl).wait_recv()
-        for d in range(1, lo_n):
-            if n >= ahead:
-                own_copy(d, sl).start()
-            fwd_copy(d, sl).start()
+        if n < ahead:
+            for d in range(1, lo_n):
+                fwd_copy(d, sl).start()
+        else:
+            send_later(sl, hi == first)
         put_left(block, sl, rhs[1 - hi, sl])
 
     def compute(u):
@@ -144,36 +165,44 @@
 
         right = jnp.concatenate([rhs[at, mine], rhs[at, theirs]], axis=1)
         high, low = halves(right)
-        for side in range(2):
+        for side in (1, 0):
             at_rows = pl.ds(side * block, block)
             value = product(lhs_high[at_rows, :], lhs_low[at_rows, :], high, low)
             kept[u, side, :block, :] = value[:, :LANES]
             given[u, side, :block, :] = value[:, LANES:]
             kept[u, side, block:, :] = summed
             given[u, side, block:, :] = summed
-        core_copy(u).start()
+            core_copy(u, side).start()
 
     def join_cores(u):
-        core_copy(u).wait_recv()
-        kept[u, 1] = kept[u, 1] + taken[u, 1]
-        swap_copy(u).start()
+        core_copy(u, 1).wait_recv()
+        for h in range(SPLIT):
+            kept[u, 1, spans[h]] = kept[u, 1, spans[h]] + taken[u, 1, spans[h]]
+            swap_copy(u, h).start()
+        core_copy(u, 0).wait_recv()
         kept[u, 0] = kept[u, 0] + taken[u, 0]
 
     def join_across(u):
         _, _, _, target, sub = place(u)
-        swap_copy(u).wait_recv()
-        value = kept[u, 0] + swapped[u]
-
-        @pl.when(target == z)
-        def _():
-            landed[z, sub] = value
-
-        @pl.when(target != z)
-        def _():
-            kept[u, 0] = value
-            z_copy(u).start()
+        for h in range(SPLIT):
+            swap_copy(u, h).wait_recv()
+            value = kept[u, 0, spans[h]] + swapped[u, spans[h]]
+
+            @pl.when(target == z)
+            def _():
+                landed[z, sub, spans[h]] = value
+
+            @pl.when(target != z)
+            def _():
+                kept[u, 0, spans[h]] = value
+                z_copy(u, h).start()
 
     def step(i, carry):
+        @pl.when(i == LATER)
+        def _():
+            for sl in order[ahead:]:
+                send_later(sl, hi != first)
+
         @pl.when(i >= 2)
         def _():
             join_across(i - 2)
@@ -190,9 +219,9 @@
     for d in range(1, z_n):
         source = lax.rem(z + d, z_n)
         for sub in range(subs):
-            copy(
-                landed.at[source, sub], landed.at[source, sub], z_send.at[0], z_recv.at[source, sub], layer(source)
-            ).wait_recv()
+            for h in range(SPLIT):
+                piece = landed.at[source, sub, spans[h]]
+                copy(piece, piece, z_send.at[0, 0], z_recv.at[source, sub, h], layer(source)).wait_recv()
     for sub in range(subs):
         value = landed[0, sub]
         for source in range(1, z_n):
@@ -205,12 +234,15 @@
             fwd_copy(d, sl).wait_send()
 
     def drain(u, carry):
-        core_copy(u).wait_send()
-        swap_copy(u).wait_send()
+        for side in range(2):
+            core_copy(u, side).wait_send()
+        for h in range(SPLIT):
+            swap_copy(u, h).wait_send()
 
         @pl.when(place(u)[3] != z)
         def _():
-            z_copy(u).wait_send()
+            for h in range(SPLIT):
+                z_copy(u, h).wait_send()
 
         return carry
 
@@ -245,8 +277,8 @@
                 pltpu.VMEM((z_n, subs) + piece, jnp.float32),
                 dma((slices,)), dma((slices,)), dma((slices,)),
                 dma((lo_n, slices)), dma((lo_n, slices)), dma((cols_n, slices)),
-                dma((units,)), dma((units,)), dma((units,)), dma((units,)), dma((units,)),
-                dma((z_n, subs)),
+                dma((units, 2)), dma((units, 2)), dma((units, SPLIT)), dma((units, SPLIT)), dma((units, SPLIT)),
+                dma((z_n, subs, SPLIT)),
             ],
             compiler_params=pltpu.CompilerParams(
                 collective_id=0, has_side_effects=True, vmem_limit_bytes=62 * 1024 * 1024

time: 109 us -> 108 us (level)
  Pallas kernels: 106 us -> 104 us
    pallas_call x1, Pallas kernels: 106 us -> 104 us  [shards(): pl.pallas_call(functools.partial(kernel, rows_n, cols_n), out_shape=jax.S...]
where the time goes in v3:
time: 108 us; the launch traced here: 107 us
  Pallas kernels  104 us (96%)
  local copies, waits for them, and re-layouts  3.16 us (3%)
    pallas_call x1, Pallas kernels, shards(): pl.pallas_call(functools.partial(kernel, rows_n, cols_n), out_shape=jax.S...  104 us

profile of v3, /device:TPU:3, one launch (start us, length us, event | category | flops | bytes accessed | tf_op | source)
XLA Modules:
  0.0 107.4 jit_solution(4234440879464081312)
XLA Ops:
  0.0 1.3 %broadcast_in_dim.3.mass_ref = f32[1,1536]{1,0:T(1,128)} reshape(f32[1536]{0:T(1024)} %param.3) | data formatting | bytes 12288 | tf_op jit(solution)/shard_map/broadcast_in_dim | solution.py:287
  1.3 104.3 %shard_map.28 = f32[512,256]{1,0:T(8,128)} custom-call(f32[1536,512]{1,0:T(8,128)} %s_ref.1, f32[1,1536]{1,0:T(1,128)} %broadcast_in_dim.3.mass_ref), custom_call_target="tpu_custom_call" | custom-call | flops 9663676416 | bytes 3145728 | tf_op jit(solution)/shard_map/pallas_call | solution.py:264
  105.6 1.9 %copy.4 = f32[512,256]{1,0:T(8,128)} copy(f32[512,256]{1,0:T(8,128)} %shard_map.28) | data formatting | bytes 1048576

commit v4 on v3

--- a/solution.py
+++ b/solution.py
@@ -203,14 +203,14 @@
             for sl in order[ahead:]:
                 send_later(sl, hi != first)
 
-        @pl.when(i >= 2)
-        def _():
-            join_across(i - 2)
-
         @pl.when(i < units)
         def _():
             compute(i)
             join_cores(i)
+
+        @pl.when(i >= 2)
+        def _():
+            join_across(i - 2)
 
         return carry
 

time: 108 us -> 107 us (level)
  no operation moved by 1% of the time
where the time goes in v4:
time: 107 us
  Pallas kernels  103 us (96%)
  local copies, waits for them, and re-layouts  3.16 us (3%)
    pallas_call x1, Pallas kernels, shards(): pl.pallas_call(functools.partial(kernel, rows_n, cols_n), out_shape=jax.S...  103 us

profile of v4, /device:TPU:3, one launch (start us, length us, event | category | flops | bytes accessed | tf_op | source)
XLA Modules:
  0.0 106.6 jit_solution(14793572774929820884)
XLA Ops:
  0.0 1.3 %broadcast_in_dim.3.mass_ref = f32[1,1536]{1,0:T(1,128)} reshape(f32[1536]{0:T(1024)} %param.3) | data formatting | bytes 12288 | tf_op jit(solution)/shard_map/broadcast_in_dim | solution.py:287
  1.3 103.4 %shard_map.28 = f32[512,256]{1,0:T(8,128)} custom-call(f32[1536,512]{1,0:T(8,128)} %s_ref.1, f32[1,1536]{1,0:T(1,128)} %broadcast_in_dim.3.mass_ref), custom_call_target="tpu_custom_call" | custom-call | flops 9663676416 | bytes 3145728 | tf_op jit(solution)/shard_map/pallas_call | solution.py:264
  104.7 1.9 %copy.4 = f32[512,256]{1,0:T(8,128)} copy(f32[512,256]{1,0:T(8,128)} %shard_map.28) | data formatting | bytes 1048576
